TPU v7x, 256 devices: a whole 4x4x8 slice. The times are simulated.
256 devices in a mesh: dp: 2 (over core), dom: 128 (over y, z, x).
Axes of the slice: x: 4, y: 4, z: 8, core: 2. Of those that a mesh axis runs over, the one named last changes fastest.
Arguments:
- features: bfloat16 [2, 49152, 512], P('dp', 'dom'), may hold values from -12 to 12
- tile_mask: int32 [2, 384, 18], P('dp', 'dom'), may hold values from 0 to 1, as said below
- cotangent: bfloat16 [2, 49152, 512], P('dp', 'dom'), may hold values from -6 to 6
- w_query: bfloat16 [512, 512], replicated, may hold values from -1 to 1
- w_key: bfloat16 [512, 512], replicated, may hold values from -1 to 1
- w_value: bfloat16 [512, 512], replicated, may hold values from -0.25 to 0.25
- w_out: bfloat16 [512, 512], replicated, may hold values from -0.25 to 0.25
Outputs:
- attended: bfloat16 [2, 49152, 512], P('dp', 'dom')
- grad_features: bfloat16 [2, 49152, 512], P('dp', 'dom')
- grad_query: float32 [512, 512], replicated
- grad_key: float32 [512, 512], replicated
- grad_value: float32 [512, 512], replicated
- grad_out: float32 [512, 512], replicated
Inputs may be any that keep to these rules, and one draw needn't show every extreme that they name: `tile_mask`: 0 or 1; the share of ones differs between tile groups, from about a quarter to all.
All inputs are finite; a program needn't handle non-finite values.
Results may differ from a plain program's by a relative error of at most 0.023.
Values may be sent and summed in bfloat16 or wider, within the bound.
A program may use at most 128 MiB of HBM per device.

v0:
```python
import jax
import jax.numpy as jnp
from jax import lax
from jax.sharding import PartitionSpec as P

HEADS = 8
HEAD_DIM = 64
TILE = 128
TILE_DEV = 3
NB = 3
CANDT = 18


def with_halo(block, sides, width):
    for axis, dim in sides:
        count = lax.axis_size(axis)
        forward = [(i, i + 1) for i in range(count - 1)]
        forward.append((count - 1, 0))
        backward = [(target, source) for source, target in forward]
        low = lax.ppermute(
            lax.slice_in_dim(block, block.shape[dim] - width, None, axis=dim), axis, forward
        )
        high = lax.ppermute(lax.slice_in_dim(block, 0, width, axis=dim), axis, backward)
        block = jnp.concatenate([low, block, high], axis=dim)
    return block


def from_partner(value, axis, distance):
    mask = 2**distance
    pairs = [(source, source ^ mask) for source in range(lax.axis_size(axis))]
    return lax.ppermute(value, axis, pairs)


def candidate_blocks(block):
    block_rows = block.shape[0]
    near = with_halo(block, (("dom", 0),), block_rows)
    pieces = [block, near[:block_rows], near[2 * block_rows :]]
    levels = lax.axis_size("dom").bit_length() - 1
    for bit_step in range(NB):
        pieces.append(from_partner(block, "dom", levels - 1 - bit_step))
    return pieces


def returned_sum(grad_parts):
    block_rows = grad_parts.shape[1]
    outgoing = jnp.concatenate([grad_parts[1], grad_parts[2]], 0)
    returned = with_halo(outgoing, (("dom", 0),), block_rows)
    summed = grad_parts[0] + returned[:block_rows] + returned[3 * block_rows :]
    levels = lax.axis_size("dom").bit_length() - 1
    for bit_step in range(NB):
        summed = summed + from_partner(grad_parts[3 + bit_step], "dom", levels - 1 - bit_step)
    return summed


def joined(stacked_parts, width_all):
    return jnp.transpose(stacked_parts, (1, 0, 2)).reshape(stacked_parts.shape[1], width_all)


def per_device(features, tile_mask, cotangent, w_query, w_key, w_value, w_out):
    node_rows = features[0]
    block_rows = node_rows.shape[0]
    width_all = node_rows.shape[1]
    highest = lax.Precision.HIGHEST
    factor = HEAD_DIM ** (-0.5)
    w_both = jnp.concatenate([w_key, w_value], 1)
    q_rows = jnp.dot(node_rows, w_query, preferred_element_type=jnp.float32).astype(jnp.bfloat16)
    kv_rows = jnp.dot(node_rows, w_both, preferred_element_type=jnp.float32).astype(jnp.bfloat16)
    cand_kv = jnp.concatenate(candidate_blocks(kv_rows), 0)
    key_count = cand_kv.shape[0]
    keys_all = cand_kv[:, :width_all]
    values_all = cand_kv[:, width_all:]
    own_tile = jnp.arange(CANDT)[None, :] == jnp.arange(TILE_DEV)[:, None]
    live_tiles = (tile_mask[0] == 1) | own_tile
    masking = jnp.where(live_tiles, 0.0, -1e30).astype(jnp.float32)
    cot_rows = cotangent[0]
    grad_o = jnp.dot(cot_rows, w_out.T, preferred_element_type=jnp.float32).astype(jnp.bfloat16)
    pair_cols = 2 * HEAD_DIM

    def head_pair(pair_index):
        col_start = pair_index * pair_cols
        q_pair = lax.dynamic_slice_in_dim(q_rows, col_start, pair_cols, 1).reshape(
            block_rows, 2, HEAD_DIM
        )
        k_pair = lax.dynamic_slice_in_dim(keys_all, col_start, pair_cols, 1).reshape(
            key_count, 2, HEAD_DIM
        )
        v_pair = lax.dynamic_slice_in_dim(values_all, col_start, pair_cols, 1).reshape(
            key_count, 2, HEAD_DIM
        )
        g_pair = lax.dynamic_slice_in_dim(grad_o, col_start, pair_cols, 1).reshape(
            block_rows, 2, HEAD_DIM
        )
        scores = (
            jnp.einsum("rhd,chd->hrc", q_pair, k_pair, preferred_element_type=jnp.float32) * factor
        )
        scores = scores.reshape(2, TILE_DEV, TILE, CANDT, TILE) + masking[None, :, None, :, None]
        scores = scores.reshape(2, block_rows, key_count)
        row_max = jnp.max(scores, axis=2, keepdims=True)
        exp_vals = jnp.exp(scores - row_max)
        prob_f32 = exp_vals / jnp.sum(exp_vals, axis=2, keepdims=True)
        prob_bf = prob_f32.astype(jnp.bfloat16)
        out_pair = jnp.einsum(
            "hrc,chd->rhd", prob_bf, v_pair, preferred_element_type=jnp.float32
        ).astype(jnp.bfloat16)
        grad_prob = jnp.einsum("rhd,chd->hrc", g_pair, v_pair, preferred_element_type=jnp.float32)
        row_delta = jnp.einsum(
            "rhd,rhd->hr", g_pair.astype(jnp.float32), out_pair.astype(jnp.float32)
        )
        grad_score = (prob_f32 * (grad_prob - row_delta[:, :, None]) * factor).astype(jnp.bfloat16)
        gq_pair = jnp.einsum(
            "hrc,chd->rhd", grad_score, k_pair, preferred_element_type=jnp.float32
        ).reshape(block_rows, pair_cols)
        gk_pair = jnp.einsum(
            "hrc,rhd->chd", grad_score, q_pair, preferred_element_type=jnp.float32
        ).reshape(key_count, pair_cols)
        gv_pair = jnp.einsum(
            "hrc,rhd->chd", prob_bf, g_pair, preferred_element_type=jnp.float32
        ).reshape(key_count, pair_cols)
        return (out_pair.reshape(block_rows, pair_cols), gq_pair, gk_pair, gv_pair)

    stacked = lax.map(head_pair, jnp.arange(HEADS // 2, dtype=jnp.int32))
    out_rows = joined(stacked[0], width_all)
    grad_q = joined(stacked[1], width_all)
    grad_k = joined(stacked[2], width_all)
    grad_v = joined(stacked[3], width_all)
    attended = jnp.dot(out_rows, w_out, preferred_element_type=jnp.float32).astype(jnp.bfloat16)
    grad_parts = jnp.concatenate([grad_k, grad_v], 1).reshape(3 + NB, block_rows, 2 * width_all)
    w_both32 = w_both.astype(jnp.float32)
    rows_f32 = node_rows.astype(jnp.float32)
    own_grad = returned_sum(grad_parts)
    kv_dx = jnp.dot(own_grad, w_both32.T, precision=highest)
    g_both = jnp.dot(rows_f32.T, own_grad, precision=highest)
    grad_x = jnp.dot(grad_q, w_query.astype(jnp.float32).T, precision=highest) + kv_dx
    g_query = jnp.dot(rows_f32.T, grad_q, precision=highest)
    g_out = jnp.dot(out_rows.T, cot_rows, preferred_element_type=jnp.float32)
    g_query, g_key, g_value, g_out = lax.psum(
        (g_query, g_both[:, :width_all], g_both[:, width_all:], g_out), ("dp", "dom")
    )
    return (attended[None], grad_x.astype(jnp.bfloat16)[None], g_query, g_key, g_value, g_out)


def solution(mesh):
    in_specs = (
        P("dp", "dom", None),
        P("dp", "dom", None),
        P("dp", "dom", None),
        P(),
        P(),
        P(),
        P(),
    )
    out_specs = (P("dp", "dom", None), P("dp", "dom", None), P(), P(), P(), P())
    return jax.shard_map(
        per_device, mesh=mesh, in_specs=in_specs, out_specs=out_specs, check_vma=False
    )
```

profile of v0, /device:TPU:8, one launch (start us, length us, event | category | flops | bytes accessed | tf_op | source)
XLA Modules:
  0.0 602.2 jit_solution(1646686012757670933)
XLA Ops:
  7.3 1.2 constant_dynamic-update-slice_fusion.5
  10.6 2.7 constant_dynamic-update-slice_fusion.11
  13.3 7.2 %collective-permute-start.4 = (bf16[384,1024]{1,0:T(8,128)(2,1)}, bf16[384,1024]{1,0:T(8,128)(2,1)S(1)}, u32[]{:S(2)}, u32[]{:S(2)}) collective-permute-start(bf16[384,1024]{1,0:T(8,128)(2,1)} %get-tuple-element.146), channel_id=1, source_target_pairs={{0,16},{1,17},{2,18},{3,19},{4,20},{5,21},{6,22},{7,23},{8,24},{9,... | collective-permute-start | bytes 2359304 | tf_op jit(solution)/shard_map/ppermute | solution.py:31
  21.0 2.6 collective-permute-start.2
  23.6 3.6 collective-permute-start.1
  28.1 45.5 %collective-permute-done = bf16[384,1024]{1,0:T(8,128)(2,1)} collective-permute-done((bf16[384,1024]{1,0:T(8,128)(2,1)}, bf16[384,1024]{1,0:T(8,128)(2,1)}, u32[]{:S(2)}, u32[]{:S(2)}) %collective-permute-start) | collective-permute-done | bytes 786464 | tf_op jit(solution)/shard_map/ppermute | solution.py:20
  73.5 2.1 constant_dynamic-update-slice_fusion.10
  75.7 2.1 constant_dynamic-update-slice_fusion.9
  77.8 2.1 constant_dynamic-update-slice_fusion.8
  79.8 2.1 constant_dynamic-update-slice_fusion.7
  82.8 4.8 fusion.33
  87.6 110.8 %while.16 = (s32[]{:T(128)}, bf16[4,384,128]{1,2,0:T(8,128)(2,1)}, f32[4,384,128]{1,2,0:T(8,128)}, f32[4,2304,128]{1,2,0:T(8,128)}, f32[4,2304,128]{1,2,0:T(8,12...) while((s32[]{:T(128)}, bf16[4,384,128]{1,2,0:T(8,128)(2,1)}, ...), condition=%wide.region_3.4_spmd, body=%wide.region_0.3_spmd.sunk | while | flops 1378665984 | bytes 104414744 | solution.py:121
  92.4 2.5 copy.50
  94.9 7.1 %fusion.93 = (f32[2,384]{1,0:T(2,128)S(1)}, f32[2,384,2304]{2,1,0:T(8,128)}) fusion(f32[384,2304]{1,0:T(8,128)} %bitcast.143, bf16[384,2,64]{0,2,1:T(8,128)(2,1)S(1)} %bitcast.150, bf16[2304,2,64]{0,2,1:T(8,128)(2,1)S(1)} %bitcast.144), kind=kOutput, calls=%fused_computation.74.clone.1 | convolution fusion | flops 233572608 | bytes 11308032 | tf_op jit(solution)/shard_map/while/body/eval_jaxpr/sub | solution.py:99
  102.0 3.8 fusion.94
  108.8 1.6 multiply_convert_fusion.2
  113.7 1.6 constant_dynamic-update-slice_fusion.17
  120.1 2.5 copy.50
  122.6 7.1 %fusion.93 = (f32[2,384]{1,0:T(2,128)S(1)}, f32[2,384,2304]{2,1,0:T(8,128)}) fusion(f32[384,2304]{1,0:T(8,128)} %bitcast.143, bf16[384,2,64]{0,2,1:T(8,128)(2,1)S(1)} %bitcast.150, bf16[2304,2,64]{0,2,1:T(8,128)(2,1)S(1)} %bitcast.144), kind=kOutput, calls=%fused_computation.74.clone.1 | convolution fusion | flops 233572608 | bytes 11308032 | tf_op jit(solution)/shard_map/while/body/eval_jaxpr/sub | solution.py:99
  129.7 3.8 fusion.94
  136.5 1.6 multiply_convert_fusion.2
  141.5 1.6 constant_dynamic-update-slice_fusion.17
  147.8 2.5 copy.50
  150.3 7.1 %fusion.93 = (f32[2,384]{1,0:T(2,128)S(1)}, f32[2,384,2304]{2,1,0:T(8,128)}) fusion(f32[384,2304]{1,0:T(8,128)} %bitcast.143, bf16[384,2,64]{0,2,1:T(8,128)(2,1)S(1)} %bitcast.150, bf16[2304,2,64]{0,2,1:T(8,128)(2,1)S(1)} %bitcast.144), kind=kOutput, calls=%fused_computation.74.clone.1 | convolution fusion | flops 233572608 | bytes 11308032 | tf_op jit(solution)/shard_map/while/body/eval_jaxpr/sub | solution.py:99
  157.4 3.8 fusion.94
  164.3 1.6 multiply_convert_fusion.2
  169.2 1.5 constant_dynamic-update-slice_fusion.17
  175.5 2.5 copy.50
  178.0 7.1 %fusion.93 = (f32[2,384]{1,0:T(2,128)S(1)}, f32[2,384,2304]{2,1,0:T(8,128)}) fusion(f32[384,2304]{1,0:T(8,128)} %bitcast.143, bf16[384,2,64]{0,2,1:T(8,128)(2,1)S(1)} %bitcast.150, bf16[2304,2,64]{0,2,1:T(8,128)(2,1)S(1)} %bitcast.144), kind=kOutput, calls=%fused_computation.74.clone.1 | convolution fusion | flops 233572608 | bytes 11308032 | tf_op jit(solution)/shard_map/while/body/eval_jaxpr/sub | solution.py:99
  185.1 3.8 fusion.94
  191.9 1.6 multiply_convert_fusion.2
  196.9 1.6 constant_dynamic-update-slice_fusion.17
  198.5 5.9 fusion.16
  204.4 6.2 %collective-permute-start.6 = (f32[384,1024]{0,1:T(8,128)}, f32[384,1024]{0,1:T(8,128)S(1)}, u32[]{:S(2)}, u32[]{:S(2)}) collective-permute-start(f32[384,1024]{0,1:T(8,128)} %get-tuple-element.137), channel_id=1, source_target_pairs={{1,0},{2,1},{3,2},{4,3},{5,4},{6,5},{7,6},{8,7},{9,8},{10,9},{11,1... | collective-permute-start | bytes 4718600 | tf_op jit(solution)/shard_map/ppermute | solution.py:23
  210.7 2.6 collective-permute-start.7
  213.2 4.3 collective-permute-start.9
  217.5 1.3 collective-permute-start.8
  218.9 1.4 fusion.23
  220.3 2.0 convolution_bitcast_fusion.1
  222.3 90.3 %collective-permute-done.5 = f32[384,1024]{0,1:T(8,128)S(1)} collective-permute-done((f32[384,1024]{0,1:T(8,128)}, f32[384,1024]{0,1:T(8,128)S(1)}, u32[]{:S(2)}, u32[]{:S(2)}) %collective-permute-start.5) | collective-permute-done | bytes 1572896 | tf_op jit(solution)/shard_map/ppermute | solution.py:20
  313.2 1.8 convolution_bitcast_fusion
  315.0 1.5 fusion.34
  317.7 2.7 fusion.38
  320.4 3.4 fusion.21
  323.8 264.0 %all-reduce.3.cloned.1.call-done = (f32[512,512]{0,1:T(8,128)}, f32[512,512]{0,1:T(8,128)}, f32[512,512]{0,1:T(8,128)}, f32[512,512]{1,0:T(8,128)}) async-done(((f32[512,512]{0,1:T(8,128)}, f32[512,512]{0,1:T(8,128)}, f32[512,512]{0,1:T(8,128)}, f32[512,512]{1,0:T(8,128)}), (f32[512,512]{0,1:T(8,128)}, f32[512,512]{0,1:T(8,128)}, f32[512,512]{0,1:T(8,128)}, ...) | async-done | bytes 4194320 | tf_op jit(solution)/shard_map/psum | solution.py:136
  587.9 2.7 copy.24
  590.5 2.5 copy.25
  593.1 1.3 copy.26
  (149 shorter events, 48.2 us)
Async XLA Ops:
  7.2 20.5 %copy-start = (bf16[512,512]{1,0:T(8,128)(2,1)S(1)}, bf16[512,512]{1,0:T(8,128)(2,1)}, u32[]{:S(2)}) copy-start(bf16[512,512]{1,0:T(8,128)(2,1)} %param.15) | copy-start | bytes 1572868
  7.2 20.0 %copy-start.4 = (bf16[1,384,512]{2,1,0:T(8,128)(2,1)S(1)}, bf16[1,384,512]{2,1,0:T(8,128)(2,1)}, u32[]{:S(2)}) copy-start(bf16[1,384,512]{2,1,0:T(8,128)(2,1)} %param.9) | copy-start | bytes 1179652
  7.2 20.0 %copy-start.6 = (bf16[512,512]{1,0:T(8,128)(2,1)S(1)}, bf16[512,512]{1,0:T(8,128)(2,1)}, u32[]{:S(2)}) copy-start(bf16[512,512]{1,0:T(8,128)(2,1)} %param.12) | copy-start | bytes 1572868
  7.2 20.4 %copy-start.14 = (s32[1,3,18]{2,0,1:T(1,128)S(1)}, s32[1,3,18]{2,0,1:T(1,128)}, u32[]{:S(2)}) copy-start(s32[1,3,18]{2,0,1:T(1,128)} %param.10) | copy-start | bytes 652
  7.2 20.4 %copy-start.9 = (bf16[1,384,512]{2,1,0:T(8,128)(2,1)S(1)}, bf16[1,384,512]{2,1,0:T(8,128)(2,1)}, u32[]{:S(2)}) copy-start(bf16[1,384,512]{2,1,0:T(8,128)(2,1)} %param.11) | copy-start | bytes 1179652
  7.2 580.6 %all-reduce.3.cloned.1.call-start = ((), (), s32[]{:S(2)}) async-start(), calls=%async_computation | async-start | bytes 8388608 | tf_op jit(solution)/shard_map/psum | solution.py:136
  9.6 1.0 copy-start.2
  13.3 68.6 %collective-permute-start.4 = (bf16[384,1024]{1,0:T(8,128)(2,1)}, bf16[384,1024]{1,0:T(8,128)(2,1)S(1)}, u32[]{:S(2)}, u32[]{:S(2)}) collective-permute-start(bf16[384,1024]{1,0:T(8,128)(2,1)} %get-tuple-element.146), channel_id=1, source_target_pairs={{0,16},{1,17},{2,18},{3,19},{4,20},{5,21},{6,22},{7,23},{8,24},{9,... | collective-permute-start | bytes 2359304 | tf_op jit(solution)/shard_map/ppermute | solution.py:31
  20.5 59.3 %collective-permute-start.3 = (bf16[384,1024]{1,0:T(8,128)(2,1)}, bf16[384,1024]{1,0:T(8,128)(2,1)}, u32[]{:S(2)}, u32[]{:S(2)}) collective-permute-start(bf16[384,1024]{1,0:T(8,128)(2,1)} %get-tuple-element.146), channel_id=1, source_target_pairs={{0,32},{1,33},{2,34},{3,35},{4,36},{5,37},{6,38},{7,39},{8,40},{9,... | collective-permute-start | bytes 2359304 | tf_op jit(solution)/shard_map/ppermute | solution.py:31
  21.0 56.8 %collective-permute-start.2 = (bf16[384,1024]{1,0:T(8,128)(2,1)}, bf16[384,1024]{1,0:T(8,128)(2,1)}, u32[]{:S(2)}, u32[]{:S(2)}) collective-permute-start(bf16[384,1024]{1,0:T(8,128)(2,1)} %get-tuple-element.146), channel_id=1, source_target_pairs={{0,64},{1,65},{2,66},{3,67},{4,68},{5,69},{6,70},{7,71},{8,72},{9,... | collective-permute-start | bytes 2359304 | tf_op jit(solution)/shard_map/ppermute | solution.py:31
  23.6 52.1 %collective-permute-start.1 = (bf16[384,1024]{1,0:T(8,128)(2,1)}, bf16[384,1024]{1,0:T(8,128)(2,1)}, u32[]{:S(2)}, u32[]{:S(2)}) collective-permute-start(bf16[384,1024]{1,0:T(8,128)(2,1)} %get-tuple-element.146), channel_id=1, source_target_pairs={{1,0},{2,1},{3,2},{4,3},{5,4},{6,5},{7,6},{8,7},{9,8},{10,9},{11,1... | collective-permute-start | bytes 2359304 | tf_op jit(solution)/shard_map/ppermute | solution.py:23
  27.2 46.4 %collective-permute-start = (bf16[384,1024]{1,0:T(8,128)(2,1)}, bf16[384,1024]{1,0:T(8,128)(2,1)}, u32[]{:S(2)}, u32[]{:S(2)}) collective-permute-start(bf16[384,1024]{1,0:T(8,128)(2,1)} %get-tuple-element.146), channel_id=1, source_target_pairs={{0,1},{1,2},{2,3},{3,4},{4,5},{5,6},{6,7},{7,8},{8,9},{9,10},{10,1... | collective-permute-start | bytes 2359304 | tf_op jit(solution)/shard_map/ppermute | solution.py:20
  87.6 1.5 copy-start.7
  105.8 3.0 copy-start.1
  112.4 3.0 copy-start.8
  115.4 1.5 copy-start.7
  133.5 3.0 copy-start.1
  140.1 3.0 copy-start.8
  143.1 1.5 copy-start.7
  161.3 3.0 copy-start.1
  167.8 2.9 copy-start.8
  170.8 1.5 copy-start.7
  188.9 3.0 copy-start.1
  195.5 2.9 copy-start.8
  198.4 114.2 %slice-start = ((s8[4718592]{0:T(1024)(128)(4,1)}), s8[4194304]{0:T(1024)(128)(4,1)S(1)}, s32[]{:S(2)}) async-start(s8[4718592]{0:T(1024)(128)(4,1)} %bitcast.156), calls=%async_computation.1 | async-start | bytes 8388608
  198.4 114.2 %slice-start.2 = ((s8[4718592]{0:T(1024)(128)(4,1)}), s8[4194304]{0:T(1024)(128)(4,1)S(1)}, s32[]{:S(2)}) async-start(s8[4718592]{0:T(1024)(128)(4,1)} %bitcast.160), calls=%async_computation.3 | async-start | bytes 8388608
  198.4 20.5 %copy-start.10 = (bf16[1,384,512]{2,1,0:T(8,128)(2,1)S(1)}, bf16[1,384,512]{2,1,0:T(8,128)(2,1)}, u32[]{:S(2)}) copy-start(bf16[1,384,512]{2,1,0:T(8,128)(2,1)} %param.11) | copy-start | bytes 1179652
  198.4 20.5 %copy-start.11 = (bf16[4,384,128]{1,2,0:T(8,128)(2,1)S(1)}, bf16[4,384,128]{1,2,0:T(8,128)(2,1)}, u32[]{:S(2)}) copy-start(bf16[4,384,128]{1,2,0:T(8,128)(2,1)} %get-tuple-element.66) | copy-start | bytes 1179652
  198.4 21.9 %copy-start.5 = (f32[4,384,128]{1,2,0:T(8,128)S(1)}, f32[4,384,128]{1,2,0:T(8,128)}, u32[]{:S(2)}) copy-start(f32[4,384,128]{1,2,0:T(8,128)} %get-tuple-element.67) | copy-start | bytes 2359300
  198.5 114.2 %slice-start.1 = ((s8[4718592]{0:T(1024)(128)(4,1)}), s8[524288]{0:T(1024)(128)(4,1)S(1)}, s32[]{:S(2)}) async-start(s8[4718592]{0:T(1024)(128)(4,1)} %bitcast.156), calls=%async_computation.2 | async-start | bytes 1048576
  198.5 114.2 %slice-start.3 = ((s8[4718592]{0:T(1024)(128)(4,1)}), s8[524288]{0:T(1024)(128)(4,1)S(1)}, s32[]{:S(2)}) async-start(s8[4718592]{0:T(1024)(128)(4,1)} %bitcast.160), calls=%async_computation.4 | async-start | bytes 1048576
  204.4 108.2 %collective-permute-start.5 = (f32[384,1024]{0,1:T(8,128)}, f32[384,1024]{0,1:T(8,128)S(1)}, u32[]{:S(2)}, u32[]{:S(2)}) collective-permute-start(f32[384,1024]{0,1:T(8,128)} %get-tuple-element.136), channel_id=1, source_target_pairs={{0,1},{1,2},{2,3},{3,4},{4,5},{5,6},{6,7},{7,8},{8,9},{9,10},{10,1... | collective-permute-start | bytes 4718600 | tf_op jit(solution)/shard_map/ppermute | solution.py:20
  204.4 108.2 %collective-permute-start.6 = (f32[384,1024]{0,1:T(8,128)}, f32[384,1024]{0,1:T(8,128)S(1)}, u32[]{:S(2)}, u32[]{:S(2)}) collective-permute-start(f32[384,1024]{0,1:T(8,128)} %get-tuple-element.137), channel_id=1, source_target_pairs={{1,0},{2,1},{3,2},{4,3},{5,4},{6,5},{7,6},{8,7},{9,8},{10,9},{11,1... | collective-permute-start | bytes 4718600 | tf_op jit(solution)/shard_map/ppermute | solution.py:23
  210.7 102.0 %collective-permute-start.7 = (f32[384,1024]{0,1:T(8,128)}, f32[384,1024]{0,1:T(8,128)S(1)}, u32[]{:S(2)}, u32[]{:S(2)}) collective-permute-start(f32[384,1024]{0,1:T(8,128)} %get-tuple-element.138), channel_id=1, source_target_pairs={{0,64},{1,65},{2,66},{3,67},{4,68},{5,69},{6,70},{7,71},{8,72},{9,... | collective-permute-start | bytes 4718600 | tf_op jit(solution)/shard_map/ppermute | solution.py:31
  213.2 99.4 %collective-permute-start.9 = (f32[384,1024]{0,1:T(8,128)S(1)}, f32[384,1024]{0,1:T(8,128)S(1)}, u32[]{:S(2)}, u32[]{:S(2)}) collective-permute-start(f32[384,1024]{0,1:T(8,128)S(1)} %get-tuple-element.139), channel_id=1, source_target_pairs={{0,16},{1,17},{2,18},{3,19},{4,20},{5,21},{6,22},{7,23},{8,24},{9,... | collective-permute-start | bytes 4718600 | tf_op jit(solution)/shard_map/ppermute | solution.py:31
  217.5 95.1 %collective-permute-start.8 = (f32[384,1024]{0,1:T(8,128)S(1)}, f32[384,1024]{0,1:T(8,128)S(1)}, u32[]{:S(2)}, u32[]{:S(2)}) collective-permute-start(f32[384,1024]{0,1:T(8,128)S(1)} %get-tuple-element.140), channel_id=1, source_target_pairs={{0,32},{1,33},{2,34},{3,35},{4,36},{5,37},{6,38},{7,39},{8,40},{9,... | collective-permute-start | bytes 4718600 | tf_op jit(solution)/shard_map/ppermute | solution.py:31
  316.5 3.9 copy-start.3
  587.9 5.2 copy-start.13
  587.9 6.5 %copy-start.12 = (f32[512,512]{1,0:T(8,128)S(1)}, f32[512,512]{1,0:T(8,128)}, u32[]{:S(2)}) copy-start(f32[512,512]{1,0:T(8,128)} %get-tuple-element.276) | copy-start | bytes 3145732
Sparse Core Ops, SparseCore 0:
  316.7 271.1 all-reduce.2
where the time goes:
time: 603 us; the launch traced here: 602 us
  waiting for transfers between devices  400 us (66%)
  local copies, waits for them, and re-layouts  68.6 us (11%)
  matrix products  66.2 us (11%)
  starting transfers between devices  28.4 us (5%)
  other arithmetic  21.8 us (4%)
  between operations  14.3 us (2%)
    psum x1, waiting for transfers between devices, per_device(): lax.psum((g_query, g_both[:, :width_all], g_both[:, width_all:], g_out),...  264 us
    ppermute x2, waiting for transfers between devices, with_halo(): lax.ppermute(lax.slice_in_dim(block, block.shape[dim] - width, None, axis...  136 us
    sub x4, matrix products, head_pair(): exp_vals = jnp.exp(scores - row_max)  28.3 us
    ppermute x6, starting transfers between devices, from_partner(): return lax.ppermute(value, axis, pairs)  18.5 us
    unnamed x41, local copies, waits for them, and re-layouts  18.1 us
    convert_element_type x4, other arithmetic, head_pair(): prob_bf = prob_f32.astype(jnp.bfloat16)  15.3 us
    while x28, local copies, waits for them, and re-layouts  14.3 us
  transfers between devices with their start and end apart: 11, of which 3 were waited for; matrix products, arithmetic and copies ran while one was open for 3% of the time, Pallas kernels for 0%

commit v1 on v0

--- a/solution.py
+++ b/solution.py
@@ -134,7 +134,7 @@
     g_query = jnp.dot(rows_f32.T, grad_q, precision=highest)
     g_out = jnp.dot(out_rows.T, cot_rows, preferred_element_type=jnp.float32)
     g_query, g_key, g_value, g_out = lax.psum(
-        (g_query, g_both[:, :width_all], g_both[:, width_all:], g_out), ("dp", "dom")
+        lax.psum((g_query, g_both[:, :width_all], g_both[:, width_all:], g_out), "dom"), "dp"
     )
     return (attended[None], grad_x.astype(jnp.bfloat16)[None], g_query, g_key, g_value, g_out)
 

time: 603 us -> 611 us (1.013)
    psum x0 -> x1, waiting for transfers between devices: none -> 33.2 us  [per_device(): lax.psum(lax.psum((g_query, g_both[:, :width_all], g_both[:, width_all:],...]
    psum x1, waiting for transfers between devices: 264 us -> 237 us  [per_device(): lax.psum((g_query, g_both[:, :width_all], g_both[:, width_all:], g_out),...]
  transfers between devices with their start and end apart: 11 -> 12, of which waited for: 3 -> 4; matrix products, arithmetic and copies ran while one was open for 3% -> 3% of each run, Pallas kernels for 0% -> 0%
where the time goes in v1:
time: 611 us; the launch traced here: 608 us
  waiting for transfers between devices  406 us (66%)
  local copies, waits for them, and re-layouts  68.5 us (11%)
  matrix products  66.3 us (11%)
  starting transfers between devices  28.4 us (5%)
  other arithmetic  21.8 us (4%)
  between operations  14.3 us (2%)
    psum x1, waiting for transfers between devices, per_device(): lax.psum((g_query, g_both[:, :width_all], g_both[:, width_all:], g_out),...  237 us
    ppermute x2, waiting for transfers between devices, with_halo(): lax.ppermute(lax.slice_in_dim(block, block.shape[dim] - width, None, axis...  136 us
    psum x1, waiting for transfers between devices, per_device(): lax.psum(lax.psum((g_query, g_both[:, :width_all], g_both[:, width_all:],...  33.2 us
    sub x4, matrix products, head_pair(): exp_vals = jnp.exp(scores - row_max)  28.4 us
    ppermute x6, starting transfers between devices, from_partner(): return lax.ppermute(value, axis, pairs)  18.5 us
    unnamed x41, local copies, waits for them, and re-layouts  18 us
    convert_element_type x4, other arithmetic, head_pair(): prob_bf = prob_f32.astype(jnp.bfloat16)  15.3 us
    while x28, local copies, waits for them, and re-layouts  14.3 us
  transfers between devices with their start and end apart: 12, of which 4 were waited for; matrix products, arithmetic and copies ran while one was open for 3% of the time, Pallas kernels for 0%

profile of v1, /device:TPU:8, one launch (start us, length us, event | category | flops | bytes accessed | tf_op | source)
XLA Modules:
  0.0 608.3 jit_solution(467972987141503662)
XLA Ops:
  10.6 2.7 constant_dynamic-update-slice_fusion.11
  13.3 7.2 %collective-permute-start.4 = (bf16[384,1024]{1,0:T(8,128)(2,1)}, bf16[384,1024]{1,0:T(8,128)(2,1)S(1)}, u32[]{:S(2)}, u32[]{:S(2)}) collective-permute-start(bf16[384,1024]{1,0:T(8,128)(2,1)} %get-tuple-element.150), channel_id=1, source_target_pairs={{0,16},{1,17},{2,18},{3,19},{4,20},{5,21},{6,22},{7,23},{8,24},{9,... | collective-permute-start | bytes 2359304 | tf_op jit(solution)/shard_map/ppermute | solution.py:31
  21.0 2.6 collective-permute-start.2
  23.5 3.6 collective-permute-start.1
  28.1 45.5 %collective-permute-done = bf16[384,1024]{1,0:T(8,128)(2,1)} collective-permute-done((bf16[384,1024]{1,0:T(8,128)(2,1)}, bf16[384,1024]{1,0:T(8,128)(2,1)}, u32[]{:S(2)}, u32[]{:S(2)}) %collective-permute-start) | collective-permute-done | bytes 786464 | tf_op jit(solution)/shard_map/ppermute | solution.py:20
  73.5 2.1 constant_dynamic-update-slice_fusion.10
  75.6 2.1 constant_dynamic-update-slice_fusion.9
  77.7 2.1 constant_dynamic-update-slice_fusion.8
  79.8 2.1 constant_dynamic-update-slice_fusion.7
  82.8 4.8 fusion.33
  87.6 110.8 %while.16 = (s32[]{:T(128)}, bf16[4,384,128]{1,2,0:T(8,128)(2,1)}, f32[4,384,128]{1,2,0:T(8,128)}, f32[4,2304,128]{1,2,0:T(8,128)}, f32[4,2304,128]{1,2,0:T(8,12...) while((s32[]{:T(128)}, bf16[4,384,128]{1,2,0:T(8,128)(2,1)}, ...), condition=%wide.region_3.4_spmd, body=%wide.region_0.3_spmd.sunk | while | flops 1378665984 | bytes 104414744 | solution.py:121
  92.3 2.5 copy.50
  94.8 7.1 %fusion.93 = (f32[2,384]{1,0:T(2,128)S(1)}, f32[2,384,2304]{2,1,0:T(8,128)}) fusion(f32[384,2304]{1,0:T(8,128)} %bitcast.143, bf16[384,2,64]{0,2,1:T(8,128)(2,1)S(1)} %bitcast.150, bf16[2304,2,64]{0,2,1:T(8,128)(2,1)S(1)} %bitcast.144), kind=kOutput, calls=%fused_computation.74.clone.1 | convolution fusion | flops 233572608 | bytes 11308032 | tf_op jit(solution)/shard_map/while/body/eval_jaxpr/sub | solution.py:99
  101.9 3.8 fusion.94
  108.7 1.6 multiply_convert_fusion.2
  113.7 1.7 constant_dynamic-update-slice_fusion.17
  120.1 2.5 copy.50
  122.6 7.1 %fusion.93 = (f32[2,384]{1,0:T(2,128)S(1)}, f32[2,384,2304]{2,1,0:T(8,128)}) fusion(f32[384,2304]{1,0:T(8,128)} %bitcast.143, bf16[384,2,64]{0,2,1:T(8,128)(2,1)S(1)} %bitcast.150, bf16[2304,2,64]{0,2,1:T(8,128)(2,1)S(1)} %bitcast.144), kind=kOutput, calls=%fused_computation.74.clone.1 | convolution fusion | flops 233572608 | bytes 11308032 | tf_op jit(solution)/shard_map/while/body/eval_jaxpr/sub | solution.py:99
  129.7 3.8 fusion.94
  136.5 1.6 multiply_convert_fusion.2
  141.5 1.6 constant_dynamic-update-slice_fusion.17
  147.8 2.5 copy.50
  150.3 7.1 %fusion.93 = (f32[2,384]{1,0:T(2,128)S(1)}, f32[2,384,2304]{2,1,0:T(8,128)}) fusion(f32[384,2304]{1,0:T(8,128)} %bitcast.143, bf16[384,2,64]{0,2,1:T(8,128)(2,1)S(1)} %bitcast.150, bf16[2304,2,64]{0,2,1:T(8,128)(2,1)S(1)} %bitcast.144), kind=kOutput, calls=%fused_computation.74.clone.1 | convolution fusion | flops 233572608 | bytes 11308032 | tf_op jit(solution)/shard_map/while/body/eval_jaxpr/sub | solution.py:99
  157.4 3.8 fusion.94
  164.3 1.6 multiply_convert_fusion.2
  169.2 1.6 constant_dynamic-update-slice_fusion.17
  175.5 2.5 copy.50
  178.0 7.1 %fusion.93 = (f32[2,384]{1,0:T(2,128)S(1)}, f32[2,384,2304]{2,1,0:T(8,128)}) fusion(f32[384,2304]{1,0:T(8,128)} %bitcast.143, bf16[384,2,64]{0,2,1:T(8,128)(2,1)S(1)} %bitcast.150, bf16[2304,2,64]{0,2,1:T(8,128)(2,1)S(1)} %bitcast.144), kind=kOutput, calls=%fused_computation.74.clone.1 | convolution fusion | flops 233572608 | bytes 11308032 | tf_op jit(solution)/shard_map/while/body/eval_jaxpr/sub | solution.py:99
  185.1 3.8 fusion.94
  191.9 1.6 multiply_convert_fusion.2
  196.9 1.5 constant_dynamic-update-slice_fusion.17
  198.5 5.9 fusion.16
  204.4 6.2 %collective-permute-start.6 = (f32[384,1024]{0,1:T(8,128)}, f32[384,1024]{0,1:T(8,128)S(1)}, u32[]{:S(2)}, u32[]{:S(2)}) collective-permute-start(f32[384,1024]{0,1:T(8,128)} %get-tuple-element.141), channel_id=1, source_target_pairs={{1,0},{2,1},{3,2},{4,3},{5,4},{6,5},{7,6},{8,7},{9,8},{10,9},{11,1... | collective-permute-start | bytes 4718600 | tf_op jit(solution)/shard_map/ppermute | solution.py:23
  210.6 2.6 collective-permute-start.7
  213.2 4.3 collective-permute-start.9
  217.6 1.3 collective-permute-start.8
  218.9 1.5 fusion.23
  220.4 2.0 convolution_bitcast_fusion.1
  222.3 90.3 %collective-permute-done.5 = f32[384,1024]{0,1:T(8,128)S(1)} collective-permute-done((f32[384,1024]{0,1:T(8,128)}, f32[384,1024]{0,1:T(8,128)S(1)}, u32[]{:S(2)}, u32[]{:S(2)}) %collective-permute-start.5) | collective-permute-done | bytes 1572896 | tf_op jit(solution)/shard_map/ppermute | solution.py:20
  313.2 1.8 convolution_bitcast_fusion
  315.1 1.5 fusion.34
  316.6 236.8 %all-reduce.5.cloned.1.call-done = (f32[512,512]{0,1:T(8,128)}, f32[512,512]{0,1:T(8,128)}, f32[512,512]{0,1:T(8,128)}, f32[512,512]{1,0:T(8,128)}) async-done(((f32[512,512]{0,1:T(8,128)}, f32[512,512]{0,1:T(8,128)}, f32[512,512]{0,1:T(8,128)}, f32[512,512]{1,0:T(8,128)}), (f32[512,512]{0,1:T(8,128)}, f32[512,512]{0,1:T(8,128)}, f32[512,512]{0,1:T(8,128)}, ...) | async-done | bytes 4194320 | tf_op jit(solution)/shard_map/psum | solution.py:137
  554.6 2.7 fusion.38
  557.3 3.4 fusion.21
  560.7 33.2 %all-reduce.7.cloned.1.call-done = (f32[512,512]{0,1:T(8,128)}, f32[512,512]{0,1:T(8,128)}, f32[512,512]{0,1:T(8,128)}, f32[512,512]{1,0:T(8,128)}) async-done(((f32[512,512]{0,1:T(8,128)}, f32[512,512]{0,1:T(8,128)}, f32[512,512]{0,1:T(8,128)}, f32[512,512]{1,0:T(8,128)}), (f32[512,512]{0,1:T(8,128)}, f32[512,512]{0,1:T(8,128)}, f32[512,512]{0,1:T(8,128)}, ...) | async-done | bytes 4194320 | tf_op jit(solution)/shard_map/psum | solution.py:136
  593.9 2.7 copy.24
  596.6 2.5 copy.25
  599.1 1.3 copy.26
  (152 shorter events, 49.4 us)
Async XLA Ops:
  7.2 20.5 %copy-start = (bf16[512,512]{1,0:T(8,128)(2,1)S(1)}, bf16[512,512]{1,0:T(8,128)(2,1)}, u32[]{:S(2)}) copy-start(bf16[512,512]{1,0:T(8,128)(2,1)} %param.15) | copy-start | bytes 1572868
  7.2 20.0 %copy-start.4 = (bf16[1,384,512]{2,1,0:T(8,128)(2,1)S(1)}, bf16[1,384,512]{2,1,0:T(8,128)(2,1)}, u32[]{:S(2)}) copy-start(bf16[1,384,512]{2,1,0:T(8,128)(2,1)} %param.9) | copy-start | bytes 1179652
  7.2 20.0 %copy-start.6 = (bf16[512,512]{1,0:T(8,128)(2,1)S(1)}, bf16[512,512]{1,0:T(8,128)(2,1)}, u32[]{:S(2)}) copy-start(bf16[512,512]{1,0:T(8,128)(2,1)} %param.12) | copy-start | bytes 1572868
  7.2 20.4 %copy-start.14 = (s32[1,3,18]{2,0,1:T(1,128)S(1)}, s32[1,3,18]{2,0,1:T(1,128)}, u32[]{:S(2)}) copy-start(s32[1,3,18]{2,0,1:T(1,128)} %param.10) | copy-start | bytes 652
  7.2 20.4 %copy-start.9 = (bf16[1,384,512]{2,1,0:T(8,128)(2,1)S(1)}, bf16[1,384,512]{2,1,0:T(8,128)(2,1)}, u32[]{:S(2)}) copy-start(bf16[1,384,512]{2,1,0:T(8,128)(2,1)} %param.11) | copy-start | bytes 1179652
  7.2 546.2 %all-reduce.5.cloned.1.call-start = ((), (), s32[]{:S(2)}) async-start(), calls=%async_computation | async-start | bytes 8388608 | tf_op jit(solution)/shard_map/psum | solution.py:137
  9.6 1.0 copy-start.2
  13.3 68.5 %collective-permute-start.4 = (bf16[384,1024]{1,0:T(8,128)(2,1)}, bf16[384,1024]{1,0:T(8,128)(2,1)S(1)}, u32[]{:S(2)}, u32[]{:S(2)}) collective-permute-start(bf16[384,1024]{1,0:T(8,128)(2,1)} %get-tuple-element.150), channel_id=1, source_target_pairs={{0,16},{1,17},{2,18},{3,19},{4,20},{5,21},{6,22},{7,23},{8,24},{9,... | collective-permute-start | bytes 2359304 | tf_op jit(solution)/shard_map/ppermute | solution.py:31
  20.5 59.3 %collective-permute-start.3 = (bf16[384,1024]{1,0:T(8,128)(2,1)}, bf16[384,1024]{1,0:T(8,128)(2,1)}, u32[]{:S(2)}, u32[]{:S(2)}) collective-permute-start(bf16[384,1024]{1,0:T(8,128)(2,1)} %get-tuple-element.150), channel_id=1, source_target_pairs={{0,32},{1,33},{2,34},{3,35},{4,36},{5,37},{6,38},{7,39},{8,40},{9,... | collective-permute-start | bytes 2359304 | tf_op jit(solution)/shard_map/ppermute | solution.py:31
  21.0 56.7 %collective-permute-start.2 = (bf16[384,1024]{1,0:T(8,128)(2,1)}, bf16[384,1024]{1,0:T(8,128)(2,1)}, u32[]{:S(2)}, u32[]{:S(2)}) collective-permute-start(bf16[384,1024]{1,0:T(8,128)(2,1)} %get-tuple-element.150), channel_id=1, source_target_pairs={{0,64},{1,65},{2,66},{3,67},{4,68},{5,69},{6,70},{7,71},{8,72},{9,... | collective-permute-start | bytes 2359304 | tf_op jit(solution)/shard_map/ppermute | solution.py:31
  23.5 52.1 %collective-permute-start.1 = (bf16[384,1024]{1,0:T(8,128)(2,1)}, bf16[384,1024]{1,0:T(8,128)(2,1)}, u32[]{:S(2)}, u32[]{:S(2)}) collective-permute-start(bf16[384,1024]{1,0:T(8,128)(2,1)} %get-tuple-element.150), channel_id=1, source_target_pairs={{1,0},{2,1},{3,2},{4,3},{5,4},{6,5},{7,6},{8,7},{9,8},{10,9},{11,1... | collective-permute-start | bytes 2359304 | tf_op jit(solution)/shard_map/ppermute | solution.py:23
  27.2 46.4 %collective-permute-start = (bf16[384,1024]{1,0:T(8,128)(2,1)}, bf16[384,1024]{1,0:T(8,128)(2,1)}, u32[]{:S(2)}, u32[]{:S(2)}) collective-permute-start(bf16[384,1024]{1,0:T(8,128)(2,1)} %get-tuple-element.150), channel_id=1, source_target_pairs={{0,1},{1,2},{2,3},{3,4},{4,5},{5,6},{6,7},{7,8},{8,9},{9,10},{10,1... | collective-permute-start | bytes 2359304 | tf_op jit(solution)/shard_map/ppermute | solution.py:20
  87.6 1.5 copy-start.7
  105.7 3.0 copy-start.1
  112.3 3.0 copy-start.8
  115.3 1.5 copy-start.7
  133.5 3.0 copy-start.1
  140.1 3.0 copy-start.8
  143.1 1.5 copy-start.7
  161.2 3.0 copy-start.1
  167.8 2.9 copy-start.8
  170.8 1.5 copy-start.7
  188.9 3.0 copy-start.1
  195.5 2.9 copy-start.8
  198.4 114.3 %slice-start = ((s8[4718592]{0:T(1024)(128)(4,1)}), s8[4194304]{0:T(1024)(128)(4,1)S(1)}, s32[]{:S(2)}) async-start(s8[4718592]{0:T(1024)(128)(4,1)} %bitcast.156), calls=%async_computation.2 | async-start | bytes 8388608
  198.4 114.3 %slice-start.2 = ((s8[4718592]{0:T(1024)(128)(4,1)}), s8[4194304]{0:T(1024)(128)(4,1)S(1)}, s32[]{:S(2)}) async-start(s8[4718592]{0:T(1024)(128)(4,1)} %bitcast.160), calls=%async_computation.4 | async-start | bytes 8388608
  198.4 20.5 %copy-start.10 = (bf16[1,384,512]{2,1,0:T(8,128)(2,1)S(1)}, bf16[1,384,512]{2,1,0:T(8,128)(2,1)}, u32[]{:S(2)}) copy-start(bf16[1,384,512]{2,1,0:T(8,128)(2,1)} %param.11) | copy-start | bytes 1179652
  198.4 20.5 %copy-start.11 = (bf16[4,384,128]{1,2,0:T(8,128)(2,1)S(1)}, bf16[4,384,128]{1,2,0:T(8,128)(2,1)}, u32[]{:S(2)}) copy-start(bf16[4,384,128]{1,2,0:T(8,128)(2,1)} %get-tuple-element.66) | copy-start | bytes 1179652
  198.4 21.9 %copy-start.5 = (f32[4,384,128]{1,2,0:T(8,128)S(1)}, f32[4,384,128]{1,2,0:T(8,128)}, u32[]{:S(2)}) copy-start(f32[4,384,128]{1,2,0:T(8,128)} %get-tuple-element.67) | copy-start | bytes 2359300
  198.4 114.2 %slice-start.1 = ((s8[4718592]{0:T(1024)(128)(4,1)}), s8[524288]{0:T(1024)(128)(4,1)S(1)}, s32[]{:S(2)}) async-start(s8[4718592]{0:T(1024)(128)(4,1)} %bitcast.156), calls=%async_computation.3 | async-start | bytes 1048576
  198.4 114.2 %slice-start.3 = ((s8[4718592]{0:T(1024)(128)(4,1)}), s8[524288]{0:T(1024)(128)(4,1)S(1)}, s32[]{:S(2)}) async-start(s8[4718592]{0:T(1024)(128)(4,1)} %bitcast.160), calls=%async_computation.5 | async-start | bytes 1048576
  204.4 108.2 %collective-permute-start.5 = (f32[384,1024]{0,1:T(8,128)}, f32[384,1024]{0,1:T(8,128)S(1)}, u32[]{:S(2)}, u32[]{:S(2)}) collective-permute-start(f32[384,1024]{0,1:T(8,128)} %get-tuple-element.140), channel_id=1, source_target_pairs={{0,1},{1,2},{2,3},{3,4},{4,5},{5,6},{6,7},{7,8},{8,9},{9,10},{10,1... | collective-permute-start | bytes 4718600 | tf_op jit(solution)/shard_map/ppermute | solution.py:20
  204.4 108.2 %collective-permute-start.6 = (f32[384,1024]{0,1:T(8,128)}, f32[384,1024]{0,1:T(8,128)S(1)}, u32[]{:S(2)}, u32[]{:S(2)}) collective-permute-start(f32[384,1024]{0,1:T(8,128)} %get-tuple-element.141), channel_id=1, source_target_pairs={{1,0},{2,1},{3,2},{4,3},{5,4},{6,5},{7,6},{8,7},{9,8},{10,9},{11,1... | collective-permute-start | bytes 4718600 | tf_op jit(solution)/shard_map/ppermute | solution.py:23
  210.6 102.0 %collective-permute-start.7 = (f32[384,1024]{0,1:T(8,128)}, f32[384,1024]{0,1:T(8,128)S(1)}, u32[]{:S(2)}, u32[]{:S(2)}) collective-permute-start(f32[384,1024]{0,1:T(8,128)} %get-tuple-element.142), channel_id=1, source_target_pairs={{0,64},{1,65},{2,66},{3,67},{4,68},{5,69},{6,70},{7,71},{8,72},{9,... | collective-permute-start | bytes 4718600 | tf_op jit(solution)/shard_map/ppermute | solution.py:31
  213.2 99.4 %collective-permute-start.9 = (f32[384,1024]{0,1:T(8,128)S(1)}, f32[384,1024]{0,1:T(8,128)S(1)}, u32[]{:S(2)}, u32[]{:S(2)}) collective-permute-start(f32[384,1024]{0,1:T(8,128)S(1)} %get-tuple-element.143), channel_id=1, source_target_pairs={{0,16},{1,17},{2,18},{3,19},{4,20},{5,21},{6,22},{7,23},{8,24},{9,... | collective-permute-start | bytes 4718600 | tf_op jit(solution)/shard_map/ppermute | solution.py:31
  217.6 95.1 %collective-permute-start.8 = (f32[384,1024]{0,1:T(8,128)S(1)}, f32[384,1024]{0,1:T(8,128)S(1)}, u32[]{:S(2)}, u32[]{:S(2)}) collective-permute-start(f32[384,1024]{0,1:T(8,128)S(1)} %get-tuple-element.144), channel_id=1, source_target_pairs={{0,32},{1,33},{2,34},{3,35},{4,36},{5,37},{6,38},{7,39},{8,40},{9,... | collective-permute-start | bytes 4718600 | tf_op jit(solution)/shard_map/ppermute | solution.py:31
  316.6 277.4 %all-reduce.7.cloned.1.call-start = ((), (), s32[]{:S(2)}) async-start(), calls=%async_computation.1 | async-start | bytes 8388608 | tf_op jit(solution)/shard_map/psum | solution.py:136
  553.4 3.9 copy-start.3
  593.9 5.2 copy-start.13
  593.9 6.5 %copy-start.12 = (f32[512,512]{1,0:T(8,128)S(1)}, f32[512,512]{1,0:T(8,128)}, u32[]{:S(2)}) copy-start(f32[512,512]{1,0:T(8,128)} %get-tuple-element.280) | copy-start | bytes 3145732
Sparse Core Ops, SparseCore 0:
  316.7 236.6 all-reduce.4
  556.7 37.1 all-reduce.6
